TPU v7x, 256 devices: a whole 4x4x8 slice. The times are simulated.
256 devices in a mesh: dp: 32 (over x, y, core), mp: 8 (over z).
Axes of the slice: x: 4, y: 4, z: 8, core: 2. Of those that a mesh axis runs over, the one named last changes fastest.
Arguments:
- queries: bfloat16 [8192, 4096], P('dp', 'mp'), may hold values from -6 to 6
- enc_rows: bfloat16 [4096, 4096], P('dp', 'mp'), may hold values from -6 to 6
- key_weight: bfloat16 [4096, 4096], P(None, 'mp'), may hold values from -0.09375 to 0.09375
- value_weight: bfloat16 [4096, 4096], P(None, 'mp'), may hold values from -0.09375 to 0.09375
- enc_len: int32 [32, 32], P('dp'), may hold values from 1 to 16, 128 in all within a row
- dec_len: int32 [32, 32], P('dp'), may hold values from 1 to 32, 256 in all within a row
- route: int32 [32, 32], P('dp'), may hold values from 0 to 31, each once within a row
- out_grad: bfloat16 [8192, 4096], P('dp', 'mp'), may hold values from -6 to 6
Outputs:
- attended: bfloat16 [8192, 4096], P('dp', 'mp')
- query_grad: bfloat16 [8192, 4096], P('dp', 'mp')
- enc_grad: bfloat16 [4096, 4096], P('dp', 'mp')
- key_weight_grad: float32 [4096, 4096], P('dp', 'mp')
- value_weight_grad: float32 [4096, 4096], P('dp', 'mp')
Inputs may be any that keep to these rules, and one draw needn't show every extreme that they name: Every row of enc_len sums to 128, and its largest entry is exactly 16. Every row of dec_len sums to 256, and its largest entry is exactly 32. Every row of route is a permutation of the data shards, so each decoder shard receives exactly one example from each shard.
All inputs are finite; a program needn't handle non-finite values.
Results may differ from a plain program's by a relative error of at most 0.013.
Values may be sent and summed in bfloat16 or wider, within the bound.
A program may use at most 128 MiB of HBM per device.

v0:
```python
import jax
import jax.numpy as jnp
from jax import lax
from jax.sharding import PartitionSpec as P

HD = 256


def attend(q_rows, g_rows, key_buf, val_buf, counts, dec_lens, slot_rows):
    rows = q_rows.shape[0]
    keys_n = key_buf.shape[0]
    heads = q_rows.shape[1] // HD
    scale = HD ** (-0.5)
    query_h = q_rows.reshape(rows, heads, HD)
    grad_h = g_rows.reshape(rows, heads, HD)
    key_h = key_buf.reshape(keys_n, heads, HD)
    val_h = val_buf.reshape(keys_n, heads, HD)
    dec_ends = jnp.cumsum(dec_lens, dtype=jnp.int32)
    dec_pos = jnp.arange(rows, dtype=jnp.int32)
    dec_source = jnp.sum(
        (dec_ends[None, :] <= dec_pos[:, None]).astype(jnp.int32), axis=1, dtype=jnp.int32
    )
    key_pos = jnp.arange(keys_n, dtype=jnp.int32)
    key_source = key_pos // slot_rows
    key_live = key_pos % slot_rows < counts[key_source]
    allowed = (dec_source[:, None] == key_source[None, :]) & key_live[None, :]
    scores = jnp.einsum("qhd,khd->hqk", query_h, key_h, preferred_element_type=jnp.float32) * scale
    scores = jnp.where(allowed[None], scores, -jnp.inf)
    top = jnp.max(scores, axis=-1, keepdims=True)
    expo = jnp.exp(scores - top)
    probs = expo / jnp.sum(expo, axis=-1, keepdims=True)
    weights = probs.astype(jnp.bfloat16)
    attended = jnp.einsum(
        "hqk,khd->qhd", weights, val_h, preferred_element_type=jnp.float32
    ).astype(jnp.bfloat16)
    dweights = jnp.einsum("qhd,khd->hqk", grad_h, val_h, preferred_element_type=jnp.float32)
    delta = jnp.sum(probs * dweights, axis=-1, keepdims=True)
    dscores = (probs * (dweights - delta) * scale).astype(jnp.bfloat16)
    query_grad = jnp.einsum(
        "hqk,khd->qhd", dscores, key_h, preferred_element_type=jnp.float32
    ).astype(jnp.bfloat16)
    key_grad = jnp.einsum(
        "hqk,qhd->khd", dscores, query_h, preferred_element_type=jnp.float32
    ).astype(jnp.bfloat16)
    value_grad = jnp.einsum(
        "hqk,qhd->khd", weights, grad_h, preferred_element_type=jnp.float32
    ).astype(jnp.bfloat16)
    width = heads * HD
    return (
        attended.reshape(rows, width),
        query_grad.reshape(rows, width),
        jnp.concatenate(
            [key_grad.reshape(keys_n, width), value_grad.reshape(keys_n, width)], axis=1
        ),
    )


def project_back(grads, key_weight, value_weight):
    width = key_weight.shape[1]
    contract_cols = (((1,), (1,)), ((), ()))
    return lax.dot_general(
        grads[:, :width], key_weight, contract_cols, preferred_element_type=jnp.float32
    ) + lax.dot_general(
        grads[:, width:], value_weight, contract_cols, preferred_element_type=jnp.float32
    )


def body(queries, enc_rows, key_weight, value_weight, enc_len, dec_len, route, out_grad):
    shards = lax.axis_size("dp")
    enc_dev = enc_rows.shape[0]
    slot_rows = 4 * enc_dev // shards
    width = key_weight.shape[1]
    model_width = key_weight.shape[0]
    lens = enc_len[0]
    targets = route[0]
    ends = jnp.cumsum(lens, dtype=jnp.int32)
    starts = ends - lens
    slots = jnp.arange(shards, dtype=jnp.int32)
    pick = targets[:, None] == slots[None, :]
    start_dest = jnp.sum(jnp.where(pick, starts[:, None], 0), axis=0, dtype=jnp.int32)
    len_dest = jnp.sum(jnp.where(pick, lens[:, None], 0), axis=0, dtype=jnp.int32)
    offsets = jnp.arange(slot_rows, dtype=jnp.int32)
    live = offsets[None, :] < len_dest[:, None]
    pack_index = jnp.where(live, start_dest[:, None] + offsets[None, :], 0).reshape(-1)
    live_flat = live.reshape(-1, 1)
    positions = jnp.arange(enc_dev, dtype=jnp.int32)
    owner = jnp.sum(
        (ends[None, :] <= positions[:, None]).astype(jnp.int32), axis=1, dtype=jnp.int32
    )
    own_pick = owner[:, None] == slots[None, :]
    dest_row = jnp.sum(jnp.where(own_pick, targets[None, :], 0), axis=1, dtype=jnp.int32)
    start_row = jnp.sum(jnp.where(own_pick, starts[None, :], 0), axis=1, dtype=jnp.int32)
    unpack_index = dest_row * slot_rows + positions - start_row
    zero_bf = jnp.zeros((), jnp.bfloat16)
    length_col = len_dest.reshape(shards, 1)
    contract_rows = (((0,), (0,)), ((), ()))
    row_buf = jnp.where(live_flat, enc_rows[pack_index], zero_bf).reshape(shards, slot_rows, -1)
    got, counts = (
        lax.all_to_all(row_buf, "dp", split_axis=0, concat_axis=0, tiled=True),
        lax.all_to_all(length_col, "dp", split_axis=0, concat_axis=0, tiled=True),
    )
    full_buf = lax.all_gather(got, "mp", axis=2, tiled=True).reshape(
        shards * slot_rows, model_width
    )
    key_buf = jnp.dot(full_buf, key_weight, preferred_element_type=jnp.float32).astype(jnp.bfloat16)
    val_buf = jnp.dot(full_buf, value_weight, preferred_element_type=jnp.float32).astype(
        jnp.bfloat16
    )
    counts = counts.reshape(shards)
    attended, query_grad, slot_grads = attend(
        queries, out_grad, key_buf, val_buf, counts, dec_len[0], slot_rows
    )
    slot_dx = project_back(slot_grads, key_weight, value_weight)
    slot_sum = lax.psum_scatter(slot_dx, "mp", scatter_dimension=1, tiled=True).astype(jnp.bfloat16)
    returned = lax.all_to_all(
        slot_sum.reshape(shards, slot_rows, -1), "dp", split_axis=0, concat_axis=0, tiled=True
    )
    enc_grad = returned.reshape(shards * slot_rows, -1)[unpack_index]
    weight_grad = lax.psum_scatter(
        lax.dot_general(full_buf, slot_grads, contract_rows, preferred_element_type=jnp.float32),
        "dp",
        scatter_dimension=0,
        tiled=True,
    )
    return (attended, query_grad, enc_grad, weight_grad[:, :width], weight_grad[:, width:])


def solution(mesh):
    in_specs = (
        P("dp", "mp"),
        P("dp", "mp"),
        P(None, "mp"),
        P(None, "mp"),
        P("dp", None),
        P("dp", None),
        P("dp", None),
        P("dp", "mp"),
    )
    out_specs = (P("dp", "mp"), P("dp", "mp"), P("dp", "mp"), P("dp", "mp"), P("dp", "mp"))
    return jax.shard_map(body, mesh=mesh, in_specs=in_specs, out_specs=out_specs, check_vma=False)
```

profile of v0, /device:TPU:32, one launch (start us, length us, event | category | flops | bytes accessed | tf_op | source)
XLA Modules:
  0.0 336.8 jit_solution(17776218580235896951)
XLA Ops:
  7.3 0.8 copy.56
  8.1 0.1 reduce
  8.2 0.7 bitcast_subtract_fusion.2
  8.9 0.8 select_reduce_fusion.3
  9.7 0.1 iota_compare_fusion.4
  9.7 0.1 add_select_fusion
  9.8 0.1 select_n.100
  9.9 2.0 gather_fusion
  11.9 0.1 broadcast_select_fusion
  12.1 18.4 %all_to_all.19 = bf16[32,16,512]{2,1,0:T(8,128)(2,1)} all-to-all(bf16[32,16,512]{2,1,0:T(8,128)(2,1)S(1)} %broadcast_select_fusion), channel_id=1, replica_groups=mesh['dp'=32,'mp'=8] {'dp'}, dimensions={0} | all-to-all | bytes 1048576 | tf_op jit(solution)/shard_map/all_to_all | solution.py:99
  30.5 0.7 copy.58
  31.2 4.1 %all-to-all-start.1 = ((s32[32,1,1]{2,1,0:T(1,128)}), s32[32,1,1]{2,1,0:T(1,128)S(1)}, u32[]{:S(2)}, u32[]{:S(2)}) async-start(s32[32,1,1]{2,1,0:T(1,128)} %copy.58), calls=%async_computation.1 | async-start | bytes 32768 | tf_op jit(solution)/shard_map/all_to_all | solution.py:100
  35.3 0.1 copy.57
  35.5 0.1 reduce.1
  35.6 0.1 copy.77
  36.6 0.2 compare_reduce_fusion
  36.8 0.1 convert_reduce_fusion
  36.9 0.1 copy.78
  37.0 5.5 %all-to-all-done.1 = s32[32,1,1]{2,1,0:T(1,128)S(1)} async-done(((s32[32,1,1]{2,1,0:T(1,128)}), s32[32,1,1]{2,1,0:T(1,128)S(1)}, u32[]{:S(2)}, u32[]{:S(2)}) %all-to-all-start.1) | async-done | bytes 160 | tf_op jit(solution)/shard_map/all_to_all | solution.py:100
  42.6 0.6 fusion.42
  43.2 0.7 fusion.41
  43.8 4.5 %compare_select_fusion.2 = s32[512,1]{0,1:T(1,128)S(1)} fusion(s32[]{:T(128)} %bitcast.34, s32[]{:T(128)} %bitcast.35, s32[]{:T(128)} %bitcast.36, s32[]{:T(128)} %bitcast.37, s32[]{:T(128)} %bitcast.38, s32[]{:T(128)} %bitcast.40, s32[]{:T(128)} %bitcast.39), kind=kLoop, calls=%fused_computation.74 | loop fusion | flops 11776 | bytes 2076 | tf_op jit(solution)/shard_map/gather | solution.py:25
  48.3 15.5 %fusion.26 = pred[512]{0:T(512)(128)(4,1)S(1)} fusion(pred[512]{0:T(512)(128)(4,1)S(1)} %compare_reduce_fusion, pred[512]{0:T(512)(128)(4,1)S(1)} %compare_reduce_fusion.1, pred[512]{0:T(512)(128)(4,1)S(1)} %compare_reduce_fusion.2, pred[512]{0:T(512)(128)(4,1)S(1)} %compare_reduce_fusion.3, pred[512]{0:T(512)(128)(4,1)S(1)} %compare_reduce_fusion.4, ...), kind=kLoop, calls=%fused_computation.95 | loop fusion | flops 16384 | bytes 15460 | tf_op jit(solution)/shard_map/lt | solution.py:25
  63.8 0.2 compare_and_fusion
  64.0 19.0 %all-gather.2.cloned.1.call-done = bf16[32,16,4096]{2,1,0:T(8,128)(2,1)} async-done(((bf16[32,16,512]{2,1,0:T(8,128)(2,1)}), bf16[32,16,4096]{2,1,0:T(8,128)(2,1)}) %all-gather.2.cloned.1.call-update) | async-done | bytes 4194320 | tf_op jit(solution)/shard_map/all_gather | solution.py:102
  83.0 6.0 %convolution_convert_fusion.2 = bf16[512,512]{0,1:T(8,128)(2,1)S(1)} fusion(bf16[512,4096]{1,0:T(8,128)(2,1)} %bitcast.141, bf16[4096,512]{1,0:T(8,128)(2,1)} %param.10), kind=kOutput, calls=%fused_computation.16 | convolution fusion | flops 2147745792 | bytes 8912896 | tf_op jit(solution)/shard_map/dot_general | solution.py:105
  89.1 2.4 convolution_convert_fusion.3
  91.4 0.3 convolution_bitcast_fusion
  91.8 1.6 fusion.43
  93.4 0.8 convolution_convert_fusion
  94.2 2.2 convolution_convert_fusion.1
  96.4 4.7 %fusion.44 = f32[512,4096]{1,0:T(8,128)S(1)} fusion(bf16[512,512]{0,1:T(8,128)(2,1)S(1)} %bitcast.123, bf16[4096,512]{1,0:T(8,128)(2,1)} %param.10), kind=kOutput, calls=%fused_computation.117 | convolution fusion | flops 2147483648 | bytes 13107200 | tf_op jit(solution)/shard_map/dot_general | solution.py:61
  101.2 6.0 %convolution_add_fusion = f32[512,4096]{1,0:T(8,128)} fusion(f32[512,4096]{1,0:T(8,128)S(1)} %fusion.44, bf16[512,512]{0,1:T(8,128)(2,1)S(1)} %bitcast.125, bf16[4096,512]{1,0:T(8,128)(2,1)S(1)} %copy-done.2), kind=kOutput, calls=%fused_computation.4 | convolution fusion | flops 2149580800 | bytes 21495808 | tf_op jit(solution)/shard_map/dot_general | solution.py:63
  107.2 11.2 %fusion.10 = f32[4096,1024]{1,0:T(8,128)} fusion(bf16[512,4096]{1,0:T(8,128)(2,1)} %bitcast.142, bf16[512,512]{0,1:T(8,128)(2,1)S(1)} %bitcast.126, bf16[512,512]{0,1:T(8,128)(2,1)S(1)} %bitcast.124), kind=kOutput, calls=%fused_computation.21 | convolution fusion | flops 4297064448 | bytes 22020096 | tf_op jit(solution)/shard_map/dot_general | solution.py:120
  118.4 0.1 convert_reduce_fusion.1
  118.5 0.6 copy-done.5
  119.1 0.1 select_reduce_fusion.1
  119.2 81.6 %reduce-scatter.3.cloned.1.call-done = f32[512,512]{1,0:T(8,128)} async-done(((f32[512,4096]{1,0:T(8,128)}), f32[512,512]{1,0:T(8,128)}) %reduce-scatter.3.cloned.1.call-update) | async-done | bytes 1048592 | tf_op jit(solution)/shard_map/reduce_scatter | solution.py:114
  200.8 2.2 convert_element_type.58
  203.0 7.1 %all-to-all-start.2 = ((bf16[32,16,512]{2,1,0:T(8,128)(2,1)}), bf16[32,16,512]{2,1,0:T(8,128)(2,1)S(1)}, u32[]{:S(2)}, u32[]{:S(2)}) async-start(bf16[32,16,512]{2,1,0:T(8,128)(2,1)} %bitcast.53), calls=%async_computation.3 | async-start | bytes 1048576 | tf_op jit(solution)/shard_map/all_to_all | solution.py:115
  210.1 0.9 convolution_convert_fusion.5
  211.0 0.8 copy.69
  211.8 2.1 convolution_convert_fusion.4
  214.0 0.8 copy.70
  214.8 6.4 %all-to-all-done.2 = bf16[32,16,512]{2,1,0:T(8,128)(2,1)S(1)} async-done(((bf16[32,16,512]{2,1,0:T(8,128)(2,1)}), bf16[32,16,512]{2,1,0:T(8,128)(2,1)S(1)}, u32[]{:S(2)}, u32[]{:S(2)}) %all-to-all-start.2) | async-done | bytes 524320 | tf_op jit(solution)/shard_map/all_to_all | solution.py:115
  221.3 1.5 gather_fusion.1
  222.8 105.6 %reduce-scatter.5.cloned.1.call-done = f32[128,1024]{1,0:T(8,128)} async-done(((f32[4096,1024]{1,0:T(8,128)}), f32[128,1024]{1,0:T(8,128)}) %reduce-scatter.5.cloned.1.call-update) | async-done | bytes 524304 | tf_op jit(solution)/shard_map/reduce_scatter | solution.py:119
  328.4 1.9 fusion.40
  (59 shorter events, 1.2 us)
Async XLA Ops:
  7.2 2.8 copy-start
  7.2 28.1 %copy-start.7 = (s32[1,32]{1,0:T(1,128)S(1)}, s32[1,32]{1,0:T(1,128)}, u32[]{:S(2)}) copy-start(s32[1,32]{1,0:T(1,128)} %param.13) | copy-start | bytes 388
  7.2 28.4 %copy-start.3 = (bf16[256,512]{1,0:T(8,128)(2,1)S(1)}, bf16[256,512]{1,0:T(8,128)(2,1)}, u32[]{:S(2)}) copy-start(bf16[256,512]{1,0:T(8,128)(2,1)} %param.8) | copy-start | bytes 786436
  7.2 29.7 %copy-start.4 = (bf16[256,512]{1,0:T(8,128)(2,1)S(1)}, bf16[256,512]{1,0:T(8,128)(2,1)}, u32[]{:S(2)}) copy-start(bf16[256,512]{1,0:T(8,128)(2,1)} %param.15) | copy-start | bytes 786436
  7.2 75.8 %all-gather.2.cloned.1.call-start = ((), (), s32[]{:S(2)}) async-start(), calls=%async_computation.5 | async-start | bytes 4718592 | tf_op jit(solution)/shard_map/all_gather | solution.py:102
  31.2 11.4 %all-to-all-start.1 = ((s32[32,1,1]{2,1,0:T(1,128)}), s32[32,1,1]{2,1,0:T(1,128)S(1)}, u32[]{:S(2)}, u32[]{:S(2)}) async-start(s32[32,1,1]{2,1,0:T(1,128)} %copy.58), calls=%async_computation.1 | async-start | bytes 32768 | tf_op jit(solution)/shard_map/all_to_all | solution.py:100
  35.3 165.6 %reduce-scatter.3.cloned.1.call-start = ((), (), s32[]{:S(2)}) async-start(), calls=%async_computation.6 | async-start | bytes 9437184 | tf_op jit(solution)/shard_map/reduce_scatter | solution.py:114
  83.0 6.0 %copy-start.1 = (bf16[4096,512]{1,0:T(8,128)(2,1)S(1)}, bf16[4096,512]{1,0:T(8,128)(2,1)}, u32[]{:S(2)}) copy-start(bf16[4096,512]{1,0:T(8,128)(2,1)} %param.11) | copy-start | bytes 12582916
  83.0 6.0 %copy-start.8 = (bf16[32,16,4096]{2,1,0:T(8,128)(2,1)S(1)}, bf16[32,16,4096]{2,1,0:T(8,128)(2,1)}, u32[]{:S(2)}) copy-start(bf16[32,16,4096]{2,1,0:T(8,128)(2,1)} %all-gather.2.cloned.1.call-done) | copy-start | bytes 12582916
  89.0 4.3 %copy-start.9 = (bf16[512,512]{0,1:T(8,128)(2,1)}, bf16[512,512]{0,1:T(8,128)(2,1)S(1)}, u32[]{:S(2)}) copy-start(bf16[512,512]{0,1:T(8,128)(2,1)S(1)} %convolution_convert_fusion.2) | copy-start | bytes 1572868
  96.4 4.8 %copy-start.2 = (bf16[4096,512]{1,0:T(8,128)(2,1)S(1)}, bf16[4096,512]{1,0:T(8,128)(2,1)}, u32[]{:S(2)}) copy-start(bf16[4096,512]{1,0:T(8,128)(2,1)} %param.11) | copy-start | bytes 12582916
  107.2 221.2 %reduce-scatter.5.cloned.1.call-start = ((), (), s32[]{:S(2)}) async-start(), calls=%async_computation.7 | async-start | bytes 17301504 | tf_op jit(solution)/shard_map/reduce_scatter | solution.py:119
  118.4 0.7 copy-start.5
  118.4 0.7 copy-start.6
  118.4 91.7 %copy-start.10 = (bf16[512,512]{0,1:T(8,128)(2,1)S(1)}, bf16[512,512]{0,1:T(8,128)(2,1)}, u32[]{:S(2)}) copy-start(bf16[512,512]{0,1:T(8,128)(2,1)} %copy-done.9) | copy-start | bytes 1572868
  203.0 18.3 %all-to-all-start.2 = ((bf16[32,16,512]{2,1,0:T(8,128)(2,1)}), bf16[32,16,512]{2,1,0:T(8,128)(2,1)S(1)}, u32[]{:S(2)}, u32[]{:S(2)}) async-start(bf16[32,16,512]{2,1,0:T(8,128)(2,1)} %bitcast.53), calls=%async_computation.3 | async-start | bytes 1048576 | tf_op jit(solution)/shard_map/all_to_all | solution.py:115
Sparse Core Ops, SparseCore 0:
  30.6 52.3 all-gather.1
  107.3 93.5 reduce-scatter.2
  205.1 123.2 reduce-scatter.4
where the time goes:
time: 338 us; the launch traced here: 337 us
  waiting for transfers between devices  218 us (64%)
  matrix products  38.2 us (11%)
  other arithmetic  25.7 us (8%)
  blocking collectives  18.4 us (5%)
  between operations  14 us (4%)
  starting transfers between devices  11.3 us (3%)
  local copies, waits for them, and re-layouts  10.9 us (3%)
    reduce_scatter x1, waiting for transfers between devices, body(): lax.psum_scatter(lax.dot_general(full_buf, slot_grads, contract_rows, pre...  106 us
    reduce_scatter x1, waiting for transfers between devices, body(): lax.psum_scatter(slot_dx, 'mp', scatter_dimension=1, tiled=True)  81.6 us
    all_gather x1, waiting for transfers between devices, body(): lax.all_gather(got, 'mp', axis=2, tiled=True)  19 us
    all_to_all x1, blocking collectives, body(): lax.all_to_all(row_buf, 'dp', split_axis=0, concat_axis=0, tiled=True)  18.4 us
    lt x1, other arithmetic, attend(): key_live = key_pos % slot_rows < counts[key_source]  15.5 us
    dot_general x1, matrix products, body(): lax.dot_general(full_buf, slot_grads, contract_rows, preferred_element_ty...  11.2 us
    all_to_all x1, starting transfers between devices, body(): lax.all_to_all(slot_sum.reshape(shards, slot_rows, -1), 'dp', split_axis=...  7.09 us
  transfers between devices with their start and end apart: 5, of which 5 were waited for; matrix products, arithmetic and copies ran while one was open for 13% of the time, Pallas kernels for 0%

commit v1 on v0

v1 whole, which is shorter than its diff:
```python
import functools

import jax
import jax.numpy as jnp
from jax import lax
from jax.experimental import pallas as pl
from jax.experimental.pallas import tpu as pltpu
from jax.sharding import PartitionSpec as P

HD = 256
ROWS = 128
DEC = 256
SLOT = 16
NDP = 32
NZ = 8
W2 = 512
DEAD = 65536.0
MESH = pl.DeviceIdType.MESH
BF = jnp.bfloat16
F32 = jnp.float32


def mm(a, b):
    return lax.dot_general(a, b, (((1,), (0,)), ((), ())), preferred_element_type=F32)


def mm_nt(a, b):
    return lax.dot_general(a, b, (((1,), (1,)), ((), ())), preferred_element_type=F32)


def mm_tn(a, b):
    return lax.dot_general(a, b, (((0,), (0,)), ((), ())), preferred_element_type=F32)


def iota(shape, dim):
    return lax.broadcasted_iota(jnp.int32, shape, dim)


def column_of(row, n):
    here = iota((n, n), 1)
    there = iota((n, n), 0)
    wide = jnp.broadcast_to(row, (n, n))
    col = jnp.sum(jnp.where(here == there, wide, 0.0), axis=1, keepdims=True)
    before = jnp.sum(jnp.where(here < there, wide, 0.0), axis=1, keepdims=True)
    return col, before


def kernel(
    q_hbm, enc_hbm, kw_hbm, vw_hbm, enc_len, dec_len, route, og_hbm,
    att_hbm, qg_hbm, eg_hbm, kwg_hbm, vwg_hbm,
    e_v, et_v, kw_v, vw_v, q_v, og_v, acc, oh_v,
    slots, kvr, gs, gr, gsend, gl, el, ps, cr, dx, rs_s, rs_r,
    att_v, qg_v, eg_v, wg_v,
    enc_sem, w_sem, q_sem, z_send, z_recv, el_send, el_recv,
    kv_send, kv_recv, g_send, g_recv, gl_send, gl_recv, c_send, c_recv,
    rs_send, rs_recv, out_sem,
):
    d = lax.axis_index("dp")
    z = lax.axis_index("mp")
    x = d // 8
    y = (d // 2) % 4
    c = d % 2
    right = (d, (z + 1) % NZ)
    left = (d, (z + NZ - 1) % NZ)
    ring = (right, left)

    def chunk_at(n):
        off = jnp.where(n % 2 == 1, NZ - (n + 1) // 2, n // 2)
        return (z + off) % NZ

    for b in range(4):
        pltpu.make_async_copy(
            enc_hbm.at[:, pl.ds(b * 128, 128)], e_v.at[z * 4 + b], enc_sem
        ).start()

    def w_copy(zc, kv):
        src, dst = ((kw_hbm, kw_v), (vw_hbm, vw_v))[kv]
        return pltpu.make_async_copy(
            src.at[pl.ds(pl.multiple_of(zc * W2, W2), W2), :], dst.at[zc], w_sem.at[zc, kv]
        )

    def load_w(n, carry):
        zc = chunk_at(n)
        w_copy(zc, 0).start()
        w_copy(zc, 1).start()
        return carry

    lax.fori_loop(0, NZ, load_w, 0)
    q_copy = pltpu.make_async_copy(q_hbm, q_v, q_sem.at[0])
    og_copy = pltpu.make_async_copy(og_hbm, og_v, q_sem.at[1])
    q_copy.start()
    og_copy.start()

    barrier = pltpu.get_barrier_semaphore()
    for peer in ring:
        pl.semaphore_signal(barrier, inc=1, device_id=peer, device_id_type=MESH)

    def greet(i, carry):
        pl.semaphore_signal(barrier, inc=1, device_id=((d + i) % NDP, z), device_id_type=MESH)
        return carry

    lax.fori_loop(1, NDP, greet, 0)

    lens_col, starts_col = column_of(enc_len[...].astype(F32), NDP)
    route_col, _ = column_of(route[...].astype(F32), NDP)
    pos = iota((NDP, ROWS), 1).astype(F32)
    inside = (pos >= starts_col) & (pos < starts_col + lens_col)
    dest = jnp.sum(
        jnp.where(inside, route_col * SLOT + pos - starts_col, 0.0), axis=0, keepdims=True
    )
    hot = iota((NDP * SLOT, ROWS), 0).astype(F32) == dest
    hot_f = jnp.where(hot, 1.0, 0.0)
    oh_v[...] = hot_f.astype(BF)

    pl.semaphore_wait(barrier, NDP + 1)
    pltpu.make_async_copy(e_v.at[pl.ds(0, 4)], e_v.at[pl.ds(z * 4, 4)], enc_sem).wait()

    def z_copy(direction, step, part):
        back = step - 1
        zc = (z + NZ - back) % NZ if direction == 0 else (z + back) % NZ
        at = pl.ds(zc * 4 + 2 * part, 2)
        return pltpu.make_async_remote_copy(
            src_ref=e_v.at[at],
            dst_ref=e_v.at[at],
            send_sem=z_send.at[direction, step - 1, part],
            recv_sem=z_recv.at[direction, step - 1, part],
            device_id=ring[direction],
            device_id_type=MESH,
        )

    for part in range(2):
        for direction in range(2):
            z_copy(direction, 1, part).start()

    def to_line(src, dst, device, here):
        @pl.when(here)
        def _():
            pltpu.make_async_copy(src, dst, el_recv).start()

        @pl.when(jnp.logical_not(here))
        def _():
            pltpu.make_async_remote_copy(
                src_ref=src, dst_ref=dst, send_sem=el_send, recv_sem=el_recv,
                device_id=device, device_id_type=MESH,
            ).start()

    acc[...] = jnp.zeros_like(acc)

    def process(zc):
        blocks = [e_v[zc * 4 + b] for b in range(4)]
        rows = jnp.concatenate(blocks, axis=1)
        w_copy(zc, 0).wait()
        w_copy(zc, 1).wait()
        acc[:, :W2] += mm(rows, kw_v[zc])
        acc[:, W2:] += mm(rows, vw_v[zc])
        for b in range(4):
            et_v[zc * 4 + b] = blocks[b].T
        xc = zc // 2
        half = zc % 2
        to_line(
            et_v.at[pl.ds(zc * 4, 4)], el.at[x * 2 + c, pl.ds(half * 4, 4)],
            (xc * 8 + y * 2, z), (xc == x) & (c == 0),
        )
        for j in range(2):
            yc = half * 2 + j
            to_line(
                et_v.at[pl.ds(zc * 4 + 2 * j, 2)], el.at[y * 2 + c, pl.ds(xc * 2, 2)],
                (x * 8 + yc * 2 + 1, z), (yc == y) & (c == 1),
            )

    process(z)

    def gather_step(k, carry):
        for part in range(2):
            for direction in range(2):
                z_copy(direction, k, part).wait_recv()
                if part == direction:
                    z_copy(direction, k + 1, part).start()
                else:
                    @pl.when(k < 3)
                    def _():
                        z_copy(direction, k + 1, part).start()
        process((z + NZ - k) % NZ)
        process((z + k) % NZ)
        return carry

    lax.fori_loop(1, 4, gather_step, 0)
    z_copy(0, 4, 0).wait_recv()
    z_copy(1, 4, 1).wait_recv()
    process((z + 4) % NZ)

    def exchange(src, dst, send_sem, recv_sem, h):
        mine = pl.ds(pl.multiple_of(d * SLOT, SLOT), SLOT)
        pltpu.make_async_copy(src.at[h, mine], dst.at[h, mine], recv_sem.at[h]).start()

        def send(i, carry):
            o = (i * 11) % NDP
            t = ((x + o // 8) % 4) * 8 + ((y + (o // 2) % 4) % 4) * 2 + (c + o % 2) % 2
            pltpu.make_async_remote_copy(
                src_ref=src.at[h, pl.ds(pl.multiple_of(t * SLOT, SLOT), SLOT)],
                dst_ref=dst.at[h, mine],
                send_sem=send_sem.at[h],
                recv_sem=recv_sem.at[h],
                device_id=(t, z),
                device_id_type=MESH,
            ).start()
            return carry

        lax.fori_loop(1, NDP, send, 0)

    def drained(buf, sem):
        pltpu.make_async_copy(buf, buf, sem).wait()

    most = pl.ds(0, (NDP - 1) * SLOT)
    hot_b = oh_v[...]
    dead = jnp.sum(hot_b.astype(F32), axis=1, keepdims=True) < 0.5
    for h in range(2):
        cols = pl.ds(h * HD, HD)
        keys = mm(hot_b, acc[:, cols].astype(BF))
        slots[h, :, :HD] = jnp.where(dead, DEAD, keys).astype(BF)
        slots[h, :, HD:] = mm(hot_b, acc[:, pl.ds(W2 + h * HD, HD)].astype(BF)).astype(BF)
        exchange(slots, kvr, kv_send, kv_recv, h)

    n_keys = NDP * SLOT
    dec_col, dec_before = column_of(dec_len[...].astype(F32), NDP)
    same = iota((NDP, n_keys), 1) // SLOT == iota((NDP, n_keys), 0)
    first = jnp.sum(jnp.where(same, dec_before, 0.0), axis=0, keepdims=True)
    last = jnp.sum(jnp.where(same, dec_before + dec_col, 0.0), axis=0, keepdims=True)
    row = iota((DEC, n_keys), 0).astype(F32)
    own = (row >= first) & (row < last)
    q_copy.wait()
    og_copy.wait()
    for h in range(2):
        cols = pl.ds(h * HD, HD)
        drained(kvr.at[h], kv_recv.at[h])
        q = q_v[:, cols]
        g = og_v[:, cols]
        k = kvr[h, :, :HD]
        v = kvr[h, :, HD:]
        total = mm_nt(jnp.ones((16, HD), BF), k)[:1]
        allowed = own & (total < 4.0e6)
        s = jnp.where(allowed, mm_nt(q, k) * (HD ** -0.5), -1e30)
        top = jnp.max(s, axis=1, keepdims=True)
        expo = jnp.exp(s - top)
        probs = expo * (1.0 / jnp.sum(expo, axis=1, keepdims=True))
        weights = probs.astype(BF)
        dw = mm_nt(g, v)
        delta = jnp.sum(probs * dw, axis=1, keepdims=True)
        ds = (probs * (dw - delta) * (HD ** -0.5)).astype(BF)
        gs[h, :, :HD] = mm_tn(ds, q).astype(BF)
        gs[h, :, HD:] = mm_tn(weights, g).astype(BF)
        exchange(gs, gr, g_send, g_recv, h)
        att_v[:, cols] = mm(weights, v).astype(BF)
        qg_v[:, cols] = mm(ds, k).astype(BF)
    att_out = pltpu.make_async_copy(att_v, att_hbm, out_sem.at[0])
    qg_out = pltpu.make_async_copy(qg_v, qg_hbm, out_sem.at[1])
    att_out.start()
    qg_out.start()

    def spread(h):
        def one(kv, i):
            if kv == 0:
                t = ((x + i) % 4) * 8 + y * 2
                at = x * 2 + c
            else:
                t = x * 8 + ((y + i) % 4) * 2 + 1
                at = y * 2 + c
            src = gsend.at[h, kv]
            dst = gl.at[h, pl.ds(pl.multiple_of(at * ROWS, ROWS), ROWS)]

            def far():
                pltpu.make_async_remote_copy(
                    src_ref=src, dst_ref=dst, send_sem=gl_send.at[h], recv_sem=gl_recv.at[h],
                    device_id=(t, z), device_id_type=MESH,
                ).start()

            if i > 0:
                far()
            else:
                pl.when(c != kv)(far)

                @pl.when(c == kv)
                def _():
                    pltpu.make_async_copy(src, dst, gl_recv.at[h]).start()

        for i in (2, 1, 3, 0):
            one(0, i)
            one(1, i)

    def unpack(h):
        drained(gr.at[h], g_recv.at[h])
        rows = mm_tn(oh_v[...], gr[h]).astype(BF)
        gsend[h, 0] = rows[:, :HD]
        gsend[h, 1] = rows[:, HD:]
        spread(h)

    def back(h, i):
        zc = i // 2
        at = pl.ds(pl.multiple_of((i % 2) * HD, HD), HD)
        cols = pl.ds(h * HD, HD)
        return mm_nt(gsend[h, 0], kw_v[zc, at, cols]) + mm_nt(gsend[h, 1], vw_v[zc, at, cols])

    def partial_blocks(h):
        drained(gl.at[h], gl_recv.at[h])

        def block(b, carry):
            lhs = jnp.concatenate([el[j, b] for j in range(8)], axis=1)
            ps[h, b] = mm(lhs, gl[h]).astype(BF)
            t = jnp.where(c == 0, x * 8 + b, (b // 2) * 8 + y * 2 + b % 2)
            dst = cr.at[h, c, jnp.where(c == 0, y, x)]

            @pl.when(t == d)
            def _():
                pltpu.make_async_copy(ps.at[h, b], dst, c_recv.at[h]).start()

            @pl.when(t != d)
            def _():
                pltpu.make_async_remote_copy(
                    src_ref=ps.at[h, b], dst_ref=dst, send_sem=c_send.at[h], recv_sem=c_recv.at[h],
                    device_id=(t, z), device_id_type=MESH,
                ).start()

            return carry

        lax.fori_loop(0, 8, block, 0)

    unpack(0)

    def back_first(i, carry):
        dx[i] = back(0, i)
        return carry

    lax.fori_loop(0, 2 * NZ, back_first, 0)
    drained(el, el_recv)
    partial_blocks(0)
    unpack(1)

    def rs_copy(direction, step, part):
        return pltpu.make_async_remote_copy(
            src_ref=rs_s.at[direction, step - 1, part],
            dst_ref=rs_r.at[direction, step - 1, part],
            send_sem=rs_send.at[direction, step - 1, part],
            recv_sem=rs_recv.at[direction, step - 1, part],
            device_id=ring[direction],
            device_id_type=MESH,
        )

    def rs_step(step):
        order = ((0, 0), (1, 1)) if step == 1 else ((0, 0), (1, 1), (0, 1), (1, 0))
        for direction, part in order:
            far = 5 - step
            zc = (z + far) % NZ if direction == 0 else (z + NZ - far) % NZ
            i = zc * 2 + part
            term = dx[i] + back(1, i)
            if step >= 3 or (step == 2 and part == direction):
                rs_copy(direction, step - 1, part).wait_recv()
                term = term + rs_r[direction, step - 2, part].astype(F32)
            rs_s[direction, step - 1, part] = term.astype(BF)
            rs_copy(direction, step, part).start()

    rs_step(1)
    partial_blocks(1)
    rs_step(2)
    rs_step(3)
    rs_step(4)

    for h in range(2):
        drained(cr.at[h], c_recv.at[h])
        cols = pl.ds(h * HD, HD)
        for kv in range(2):
            total = cr[h, kv, 0].astype(F32)
            for j in range(1, 4):
                total = total + cr[h, kv, j].astype(F32)
            wg_v[kv, :, cols] = total
    kwg_out = pltpu.make_async_copy(wg_v.at[0], kwg_hbm, out_sem.at[2])
    vwg_out = pltpu.make_async_copy(wg_v.at[1], vwg_hbm, out_sem.at[3])
    kwg_out.start()
    vwg_out.start()
    for part in range(2):
        i = z * 2 + part
        total = dx[i] + back(1, i)
        for direction in range(2):
            rs_copy(direction, 4, part).wait_recv()
            total = total + rs_r[direction, 3, part].astype(F32)
        eg_v[:, pl.ds(part * HD, HD)] = total.astype(BF)
    eg_out = pltpu.make_async_copy(eg_v, eg_hbm, out_sem.at[4])
    eg_out.start()

    for direction in range(2):
        for step in range(1, 5):
            for part in range(2):
                if step < 4 or part == direction:
                    z_copy(direction, step, part).wait_send()
                if step > 1 or part == direction:
                    rs_copy(direction, step, part).wait_send()
    drained(el.at[pl.ds(0, 7)], el_send)
    for h in range(2):
        drained(kvr.at[h, most], kv_send.at[h])
        drained(gr.at[h, most], g_send.at[h])
        drained(gl.at[h, pl.ds(0, 7 * ROWS)], gl_send.at[h])
        drained(ps.at[h, pl.ds(0, 7)], c_send.at[h])
    att_out.wait()
    qg_out.wait()
    kwg_out.wait()
    vwg_out.wait()
    eg_out.wait()


def body(queries, enc_rows, key_weight, value_weight, enc_len, dec_len, route, out_grad):
    any_spec = pl.BlockSpec(memory_space=pl.ANY)
    small = pl.BlockSpec(memory_space=pltpu.VMEM)
    dma = pltpu.SemaphoreType.DMA
    return pl.pallas_call(
        kernel,
        out_shape=(
            jax.ShapeDtypeStruct((DEC, W2), BF),
            jax.ShapeDtypeStruct((DEC, W2), BF),
            jax.ShapeDtypeStruct((ROWS, W2), BF),
            jax.ShapeDtypeStruct((ROWS, W2), F32),
            jax.ShapeDtypeStruct((ROWS, W2), F32),
        ),
        in_specs=[any_spec] * 4 + [small] * 3 + [any_spec],
        out_specs=[any_spec] * 5,
        scratch_shapes=[
            pltpu.VMEM((32, 128, 128), BF),
            pltpu.VMEM((32, 128, 128), BF),
            pltpu.VMEM((NZ, W2, W2), BF),
            pltpu.VMEM((NZ, W2, W2), BF),
            pltpu.VMEM((DEC, W2), BF),
            pltpu.VMEM((DEC, W2), BF),
            pltpu.VMEM((ROWS, 2 * W2), F32),
            pltpu.VMEM((NDP * SLOT, ROWS), BF),
            pltpu.VMEM((2, NDP * SLOT, W2), BF),
            pltpu.VMEM((2, NDP * SLOT, W2), BF),
            pltpu.VMEM((2, NDP * SLOT, W2), BF),
            pltpu.VMEM((2, NDP * SLOT, W2), BF),
            pltpu.VMEM((2, 2, ROWS, HD), BF),
            pltpu.VMEM((2, 8 * ROWS, HD), BF),
            pltpu.VMEM((8, 8, 128, 128), BF),
            pltpu.VMEM((2, 8, 128, HD), BF),
            pltpu.VMEM((2, 2, 4, 128, HD), BF),
            pltpu.VMEM((2 * NZ, ROWS, HD), F32),
            pltpu.VMEM((2, 4, 2, ROWS, HD), BF),
            pltpu.VMEM((2, 4, 2, ROWS, HD), BF),
            pltpu.VMEM((DEC, W2), BF),
            pltpu.VMEM((DEC, W2), BF),
            pltpu.VMEM((ROWS, W2), BF),
            pltpu.VMEM((2, ROWS, W2), F32),
            dma(()),
            dma((NZ, 2)),
            dma((2,)),
            dma((2, 4, 2)),
            dma((2, 4, 2)),
            dma(()),
            dma(()),
            dma((2,)),
            dma((2,)),
            dma((2,)),
            dma((2,)),
            dma((2,)),
            dma((2,)),
            dma((2,)),
            dma((2,)),
            dma((2, 4, 2)),
            dma((2, 4, 2)),
            dma((5,)),
        ],
        compiler_params=pltpu.CompilerParams(
            collective_id=0, has_side_effects=True, vmem_limit_bytes=48 * 1024 * 1024
        ),
    )(queries, enc_rows, key_weight, value_weight, enc_len, dec_len, route, out_grad)


def solution(mesh):
    in_specs = (
        P("dp", "mp"),
        P("dp", "mp"),
        P(None, "mp"),
        P(None, "mp"),
        P("dp", None),
        P("dp", None),
        P("dp", None),
        P("dp", "mp"),
    )
    out_specs = (P("dp", "mp"), P("dp", "mp"), P("dp", "mp"), P("dp", "mp"), P("dp", "mp"))
    return jax.shard_map(body, mesh=mesh, in_specs=in_specs, out_specs=out_specs, check_vma=False)
```

time: 338 us -> 101 us (0.30)
  the two profiles are of different devices: /device:TPU:32 before, /device:TPU:1 now
where the time goes in v1:
time: 101 us
  Pallas kernels  90 us (89%)
  local copies, waits for them, and re-layouts  10.4 us (10%)
    pallas_call x1, Pallas kernels, body(): pl.pallas_call(kernel, out_shape=(jax.ShapeDtypeStruct((DEC, W2), BF), ja...  90 us
    unnamed x19, local copies, waits for them, and re-layouts  10.4 us

profile of v1, /device:TPU:1, one launch (start us, length us, event | category | flops | bytes accessed | tf_op | source)
XLA Modules:
  0.0 101.1 jit_solution(17964841126967545253)
XLA Ops:
  0.6 0.0 copy-start
  0.6 2.2 %copy-done = bf16[4096,512]{1,0:T(8,128)(2,1)S(1)} copy-done((bf16[4096,512]{1,0:T(8,128)(2,1)S(1)}, bf16[4096,512]{1,0:T(8,128)(2,1)}, u32[]{:S(2)}) %copy-start) | copy-done | bytes 4194328
  2.8 0.0 copy-start.1
  2.8 0.9 copy-done.1
  3.8 0.0 copy-start.2
  3.8 0.9 copy-done.2
  4.7 0.0 copy-start.3
  4.7 0.9 copy-done.3
  5.6 0.0 copy-start.4
  5.6 0.7 copy-done.4
  6.3 0.0 copy-start.5
  6.3 0.7 copy-done.5
  6.9 0.0 copy-start.6
  6.9 0.7 copy-done.6
  7.6 90.0 %shard_map.119 = (bf16[256,512]{1,0:T(8,128)(2,1)S(1)}, bf16[256,512]{1,0:T(8,128)(2,1)S(1)}, bf16[128,512]{1,0:T(8,128)(2,1)S(1)}, f32[128,512]{1,0:T(8,128)S(1)}, f32[128,512]{1,0:T(8,128)S(1)}) custom-call(bf16[256,512]{1,0:T(8,128)(2,1)S(1)} %copy-done.1, bf16[128,512]{1,0:T(8,128)(2,1)S(1)} %copy-done.3, bf16[4096,512]{1,0:T(8,128)(2,1)S(1)} %copy-done, ...), custom_call_target="tpu_custom_call" | custom-call | tf_op jit(solution)/shard_map/pallas_call | solution.py:413
  97.6 0.7 copy.18
  98.3 0.7 copy.19
  99.0 0.7 copy.20
  99.7 0.7 copy.21
  100.4 0.7 copy.22
Async XLA Ops:
  0.6 2.2 %copy-start = (bf16[4096,512]{1,0:T(8,128)(2,1)S(1)}, bf16[4096,512]{1,0:T(8,128)(2,1)}, u32[]{:S(2)}) copy-start(bf16[4096,512]{1,0:T(8,128)(2,1)} %kw_hbm.1) | copy-start | bytes 12582916
  2.8 0.9 copy-start.1
  3.8 0.9 copy-start.2
  4.7 0.9 copy-start.3
  5.6 0.7 copy-start.4
  6.3 0.7 copy-start.5
  6.9 0.7 copy-start.6

commit v2 on v1

--- a/solution.py
+++ b/solution.py
@@ -1,5 +1,3 @@
-import functools
-
 import jax
 import jax.numpy as jnp
 from jax import lax
@@ -118,7 +116,7 @@
     def z_copy(direction, step, part):
         back = step - 1
         zc = (z + NZ - back) % NZ if direction == 0 else (z + back) % NZ
-        at = pl.ds(zc * 4 + 2 * part, 2)
+        at = zc * 4 + part
         return pltpu.make_async_remote_copy(
             src_ref=e_v.at[at],
             dst_ref=e_v.at[at],
@@ -128,9 +126,12 @@
             device_id_type=MESH,
         )
 
-    for part in range(2):
-        for direction in range(2):
-            z_copy(direction, 1, part).start()
+    def near(direction, part):
+        return (part < 2) == (direction == 0)
+
+    travel = ((0, 0), (1, 3), (0, 1), (1, 2), (0, 2), (1, 1), (0, 3), (1, 0))
+    for direction, part in travel:
+        z_copy(direction, 1, part).start()
 
     def to_line(src, dst, device, here):
         @pl.when(here)
@@ -171,22 +172,19 @@
     process(z)
 
     def gather_step(k, carry):
-        for part in range(2):
-            for direction in range(2):
-                z_copy(direction, k, part).wait_recv()
-                if part == direction:
-                    z_copy(direction, k + 1, part).start()
-                else:
-                    @pl.when(k < 3)
-                    def _():
-                        z_copy(direction, k + 1, part).start()
+        for direction, part in travel:
+            z_copy(direction, k, part).wait_recv()
+            if near(direction, part):
+                z_copy(direction, k + 1, part).start()
+            else:
+                pl.when(k < 3)(z_copy(direction, k + 1, part).start)
         process((z + NZ - k) % NZ)
         process((z + k) % NZ)
         return carry
 
     lax.fori_loop(1, 4, gather_step, 0)
-    z_copy(0, 4, 0).wait_recv()
-    z_copy(1, 4, 1).wait_recv()
+    for direction, part in travel[:4]:
+        z_copy(direction, 4, part).wait_recv()
     process((z + 4) % NZ)
 
     def exchange(src, dst, send_sem, recv_sem, h):
@@ -294,11 +292,9 @@
         gsend[h, 1] = rows[:, HD:]
         spread(h)
 
-    def back(h, i):
-        zc = i // 2
-        at = pl.ds(pl.multiple_of((i % 2) * HD, HD), HD)
+    def back(h, zc):
         cols = pl.ds(h * HD, HD)
-        return mm_nt(gsend[h, 0], kw_v[zc, at, cols]) + mm_nt(gsend[h, 1], vw_v[zc, at, cols])
+        return mm_nt(gsend[h, 0], kw_v[zc, :, cols]) + mm_nt(gsend[h, 1], vw_v[zc, :, cols])
 
     def partial_blocks(h):
         drained(gl.at[h], gl_recv.at[h])
@@ -326,13 +322,11 @@
 
     unpack(0)
 
-    def back_first(i, carry):
-        dx[i] = back(0, i)
+    def back_first(zc, carry):
+        dx[zc] = back(0, zc)
         return carry
 
-    lax.fori_loop(0, 2 * NZ, back_first, 0)
-    drained(el, el_recv)
-    partial_blocks(0)
+    lax.fori_loop(0, NZ, back_first, 0)
     unpack(1)
 
     def rs_copy(direction, step, part):
@@ -345,24 +339,37 @@
             device_id_type=MESH,
         )
 
-    def rs_step(step):
-        order = ((0, 0), (1, 1)) if step == 1 else ((0, 0), (1, 1), (0, 1), (1, 0))
-        for direction, part in order:
-            far = 5 - step
-            zc = (z + far) % NZ if direction == 0 else (z + NZ - far) % NZ
-            i = zc * 2 + part
-            term = dx[i] + back(1, i)
-            if step >= 3 or (step == 2 and part == direction):
-                rs_copy(direction, step - 1, part).wait_recv()
-                term = term + rs_r[direction, step - 2, part].astype(F32)
-            rs_s[direction, step - 1, part] = term.astype(BF)
-            rs_copy(direction, step, part).start()
-
-    rs_step(1)
+    def rs_part(step, direction, part):
+        far = 5 - step
+        zc = (z + far) % NZ if direction == 0 else (z + NZ - far) % NZ
+        term = dx[zc, :, pl.ds(part * 128, 128)]
+        if step >= 3 or (step == 2 and near(direction, part)):
+            rs_copy(direction, step - 1, part).wait_recv()
+            term = term + rs_r[direction, step - 2, part].astype(F32)
+        rs_s[direction, step - 1, part] = term.astype(BF)
+        rs_copy(direction, step, part).start()
+
+    def back_second(n, carry):
+        zc = chunk_at(7 - n)
+        dx[zc] += back(1, zc)
+        return carry
+
+    first_parts, last_parts = travel[:4], travel[4:]
+    lax.fori_loop(0, 1, back_second, 0)
+    for direction, part in first_parts:
+        rs_part(1, direction, part)
+    lax.fori_loop(1, 3, back_second, 0)
+    for direction, part in last_parts:
+        rs_part(2, direction, part)
+    lax.fori_loop(3, NZ, back_second, 0)
+    drained(el, el_recv)
+    partial_blocks(0)
+    for direction, part in first_parts:
+        rs_part(2, direction, part)
     partial_blocks(1)
-    rs_step(2)
-    rs_step(3)
-    rs_step(4)
+    for step in (3, 4):
+        for direction, part in last_parts + first_parts:
+            rs_part(step, direction, part)
 
     for h in range(2):
         drained(cr.at[h], c_recv.at[h])
@@ -376,22 +383,22 @@
     vwg_out = pltpu.make_async_copy(wg_v.at[1], vwg_hbm, out_sem.at[3])
     kwg_out.start()
     vwg_out.start()
-    for part in range(2):
-        i = z * 2 + part
-        total = dx[i] + back(1, i)
+    for part in (2, 1, 3, 0):
+        cols = pl.ds(part * 128, 128)
+        total = dx[z, :, cols]
         for direction in range(2):
             rs_copy(direction, 4, part).wait_recv()
             total = total + rs_r[direction, 3, part].astype(F32)
-        eg_v[:, pl.ds(part * HD, HD)] = total.astype(BF)
+        eg_v[:, cols] = total.astype(BF)
     eg_out = pltpu.make_async_copy(eg_v, eg_hbm, out_sem.at[4])
     eg_out.start()
 
     for direction in range(2):
         for step in range(1, 5):
-            for part in range(2):
-                if step < 4 or part == direction:
+            for part in range(4):
+                if step < 4 or near(direction, part):
                     z_copy(direction, step, part).wait_send()
-                if step > 1 or part == direction:
+                if step > 1 or near(direction, part):
                     rs_copy(direction, step, part).wait_send()
     drained(el.at[pl.ds(0, 7)], el_send)
     for h in range(2):
@@ -406,19 +413,33 @@
     eg_out.wait()
 
 
+def hand_over(*refs):
+    given, results, held, sems = refs[:5], refs[5:10], refs[10:15], refs[15]
+    inward = [pltpu.make_async_copy(given[i], held[i], sems.at[0, i]) for i in range(5)]
+    outward = [pltpu.make_async_copy(held[i], results[i], sems.at[1, i]) for i in range(5)]
+    for copy in inward:
+        copy.start()
+    for i in range(5):
+        inward[i].wait()
+        outward[i].start()
+    for copy in outward:
+        copy.wait()
+
+
 def body(queries, enc_rows, key_weight, value_weight, enc_len, dec_len, route, out_grad):
     any_spec = pl.BlockSpec(memory_space=pl.ANY)
     small = pl.BlockSpec(memory_space=pltpu.VMEM)
     dma = pltpu.SemaphoreType.DMA
-    return pl.pallas_call(
+    results = (
+        jax.ShapeDtypeStruct((DEC, W2), BF),
+        jax.ShapeDtypeStruct((DEC, W2), BF),
+        jax.ShapeDtypeStruct((ROWS, W2), BF),
+        jax.ShapeDtypeStruct((ROWS, W2), F32),
+        jax.ShapeDtypeStruct((ROWS, W2), F32),
+    )
+    made = pl.pallas_call(
         kernel,
-        out_shape=(
-            jax.ShapeDtypeStruct((DEC, W2), BF),
-            jax.ShapeDtypeStruct((DEC, W2), BF),
-            jax.ShapeDtypeStruct((ROWS, W2), BF),
-            jax.ShapeDtypeStruct((ROWS, W2), F32),
-            jax.ShapeDtypeStruct((ROWS, W2), F32),
-        ),
+        out_shape=results,
         in_specs=[any_spec] * 4 + [small] * 3 + [any_spec],
         out_specs=[any_spec] * 5,
         scratch_shapes=[
@@ -439,9 +460,9 @@
             pltpu.VMEM((8, 8, 128, 128), BF),
             pltpu.VMEM((2, 8, 128, HD), BF),
             pltpu.VMEM((2, 2, 4, 128, HD), BF),
-            pltpu.VMEM((2 * NZ, ROWS, HD), F32),
-            pltpu.VMEM((2, 4, 2, ROWS, HD), BF),
-            pltpu.VMEM((2, 4, 2, ROWS, HD), BF),
+            pltpu.VMEM((NZ, ROWS, W2), F32),
+            pltpu.VMEM((2, 4, 4, ROWS, 128), BF),
+            pltpu.VMEM((2, 4, 4, ROWS, 128), BF),
             pltpu.VMEM((DEC, W2), BF),
             pltpu.VMEM((DEC, W2), BF),
             pltpu.VMEM((ROWS, W2), BF),
@@ -449,8 +470,8 @@
             dma(()),
             dma((NZ, 2)),
             dma((2,)),
-            dma((2, 4, 2)),
-            dma((2, 4, 2)),
+            dma((2, 4, 4)),
+            dma((2, 4, 4)),
             dma(()),
             dma(()),
             dma((2,)),
@@ -461,14 +482,22 @@
             dma((2,)),
             dma((2,)),
             dma((2,)),
-            dma((2, 4, 2)),
-            dma((2, 4, 2)),
+            dma((2, 4, 4)),
+            dma((2, 4, 4)),
             dma((5,)),
         ],
         compiler_params=pltpu.CompilerParams(
-            collective_id=0, has_side_effects=True, vmem_limit_bytes=48 * 1024 * 1024
+            collective_id=0, has_side_effects=True, vmem_limit_bytes=60 * 1024 * 1024
         ),
     )(queries, enc_rows, key_weight, value_weight, enc_len, dec_len, route, out_grad)
+    return pl.pallas_call(
+        hand_over,
+        out_shape=results,
+        in_specs=[any_spec] * 5,
+        out_specs=[any_spec] * 5,
+        scratch_shapes=[pltpu.VMEM(r.shape, r.dtype) for r in results] + [dma((2, 5))],
+        compiler_params=pltpu.CompilerParams(vmem_limit_bytes=60 * 1024 * 1024),
+    )(*made)
 
 
 def solution(mesh):

time: 101 us -> 83.8 us (0.83)
  the two profiles are of different devices: /device:TPU:1 before, /device:TPU:32 now
where the time goes in v2:
time: 83.8 us; the launch traced here: 82.8 us
  Pallas kernels  82.1 us (98%)
    pallas_call x1, Pallas kernels, body(): pl.pallas_call(kernel, out_shape=results, in_specs=[any_spec] * 4 + [smal...  80.1 us
    pallas_call x1, Pallas kernels, body(): pl.pallas_call(hand_over, out_shape=results, in_specs=[any_spec] * 5, out...  2.04 us

profile of v2, /device:TPU:32, one launch (start us, length us, event | category | flops | bytes accessed | tf_op | source)
XLA Modules:
  0.0 82.8 jit_solution(15591655188887458098)
XLA Ops:
  0.6 80.1 %shard_map.119 = (bf16[256,512]{1,0:T(8,128)(2,1)}, bf16[256,512]{1,0:T(8,128)(2,1)}, bf16[128,512]{1,0:T(8,128)(2,1)}, f32[128,512]{1,0:T(8,128)}, f32[128,512]{1,0:T(8,128)}) custom-call(bf16[256,512]{1,0:T(8,128)(2,1)} %q_hbm.1, bf16[128,512]{1,0:T(8,128)(2,1)} %enc_hbm.1, bf16[4096,512]{1,0:T(8,128)(2,1)} %kw_hbm.1, bf16[4096,512]{1,0:T(8,128)(2,1)} %vw_hbm.1, ...), custom_call_target="tpu_custom_call" | custom-call | tf_op jit(solution)/shard_map/pallas_call | solution.py:440
  80.7 2.0 %shard_map.120 = (bf16[256,512]{1,0:T(8,128)(2,1)}, bf16[256,512]{1,0:T(8,128)(2,1)}, bf16[128,512]{1,0:T(8,128)(2,1)}, f32[128,512]{1,0:T(8,128)}, f32[128,512]{1,0:T(8,128)}) custom-call(bf16[256,512]{1,0:T(8,128)(2,1)} %get-tuple-element.10.refs_0_, bf16[256,512]{1,0:T(8,128)(2,1)} %get-tuple-element.11.refs_1_, ...), custom_call_target="tpu_custom_call" | custom-call | tf_op jit(solution)/shard_map/pallas_call | solution.py:493

commit v3 on v2

--- a/solution.py
+++ b/solution.py
@@ -12,6 +12,7 @@
 NDP = 32
 NZ = 8
 W2 = 512
+FAR = 3
 DEAD = 65536.0
 MESH = pl.DeviceIdType.MESH
 BF = jnp.bfloat16
@@ -44,14 +45,14 @@
 
 
 def kernel(
-    q_hbm, enc_hbm, kw_hbm, vw_hbm, enc_len, dec_len, route, og_hbm,
+    q_hbm, enc_hbm, kw_hbm, vw_hbm, enc_len_hbm, dec_len_hbm, route_hbm, og_hbm,
     att_hbm, qg_hbm, eg_hbm, kwg_hbm, vwg_hbm,
     e_v, et_v, kw_v, vw_v, q_v, og_v, acc, oh_v,
     slots, kvr, gs, gr, gsend, gl, el, ps, cr, dx, rs_s, rs_r,
-    att_v, qg_v, eg_v, wg_v,
-    enc_sem, w_sem, q_sem, z_send, z_recv, el_send, el_recv,
+    att_v, qg_v, eg_v, wg_v, enc_len, dec_len, route,
+    enc_sem, w_sem, q_sem, z_send, z_recv, el_send, el_recv, elz_send,
     kv_send, kv_recv, g_send, g_recv, gl_send, gl_recv, c_send, c_recv,
-    rs_send, rs_recv, out_sem,
+    rs_send, rs_recv, out_sem, int_sem,
 ):
     d = lax.axis_index("dp")
     z = lax.axis_index("mp")
@@ -66,10 +67,23 @@
         off = jnp.where(n % 2 == 1, NZ - (n + 1) // 2, n // 2)
         return (z + off) % NZ
 
+    def drained(buf, sem):
+        pltpu.make_async_copy(buf, buf, sem).wait()
+
     for b in range(4):
         pltpu.make_async_copy(
             enc_hbm.at[:, pl.ds(b * 128, 128)], e_v.at[z * 4 + b], enc_sem
         ).start()
+
+    barrier = pltpu.get_barrier_semaphore()
+    for peer in ring:
+        pl.semaphore_signal(barrier, inc=1, device_id=peer, device_id_type=MESH)
+
+    def greet(i, carry):
+        pl.semaphore_signal(barrier, inc=1, device_id=((d + i) % NDP, z), device_id_type=MESH)
+        return carry
+
+    lax.fori_loop(1, NDP, greet, 0)
 
     def w_copy(zc, kv):
         src, dst = ((kw_hbm, kw_v), (vw_hbm, vw_v))[kv]
@@ -88,27 +102,14 @@
     og_copy = pltpu.make_async_copy(og_hbm, og_v, q_sem.at[1])
     q_copy.start()
     og_copy.start()
-
-    barrier = pltpu.get_barrier_semaphore()
-    for peer in ring:
-        pl.semaphore_signal(barrier, inc=1, device_id=peer, device_id_type=MESH)
-
-    def greet(i, carry):
-        pl.semaphore_signal(barrier, inc=1, device_id=((d + i) % NDP, z), device_id_type=MESH)
-        return carry
-
-    lax.fori_loop(1, NDP, greet, 0)
-
-    lens_col, starts_col = column_of(enc_len[...].astype(F32), NDP)
-    route_col, _ = column_of(route[...].astype(F32), NDP)
-    pos = iota((NDP, ROWS), 1).astype(F32)
-    inside = (pos >= starts_col) & (pos < starts_col + lens_col)
-    dest = jnp.sum(
-        jnp.where(inside, route_col * SLOT + pos - starts_col, 0.0), axis=0, keepdims=True
-    )
-    hot = iota((NDP * SLOT, ROWS), 0).astype(F32) == dest
-    hot_f = jnp.where(hot, 1.0, 0.0)
-    oh_v[...] = hot_f.astype(BF)
+    int_copies = [
+        pltpu.make_async_copy(src, dst, int_sem.at[i])
+        for i, (src, dst) in enumerate(
+            ((enc_len_hbm, enc_len), (route_hbm, route), (dec_len_hbm, dec_len))
+        )
+    ]
+    for copy in int_copies:
+        copy.start()
 
     pl.semaphore_wait(barrier, NDP + 1)
     pltpu.make_async_copy(e_v.at[pl.ds(0, 4)], e_v.at[pl.ds(z * 4, 4)], enc_sem).wait()
@@ -133,17 +134,30 @@
     for direction, part in travel:
         z_copy(direction, 1, part).start()
 
-    def to_line(src, dst, device, here):
+    def to_line(zc, src, dst, device, here):
         @pl.when(here)
         def _():
-            pltpu.make_async_copy(src, dst, el_recv).start()
+            pltpu.make_async_copy(src, dst, el_recv.at[zc]).start()
 
         @pl.when(jnp.logical_not(here))
         def _():
             pltpu.make_async_remote_copy(
-                src_ref=src, dst_ref=dst, send_sem=el_send, recv_sem=el_recv,
+                src_ref=src, dst_ref=dst, send_sem=el_send.at[zc], recv_sem=el_recv.at[zc],
                 device_id=device, device_id_type=MESH,
             ).start()
+
+    int_copies[0].wait()
+    int_copies[1].wait()
+    lens_col, starts_col = column_of(enc_len[...].astype(F32), NDP)
+    route_col, _ = column_of(route[...].astype(F32), NDP)
+    pos = iota((NDP, ROWS), 1).astype(F32)
+    inside = (pos >= starts_col) & (pos < starts_col + lens_col)
+    dest = jnp.sum(
+        jnp.where(inside, route_col * SLOT + pos - starts_col, 0.0), axis=0, keepdims=True
+    )
+    hot = iota((NDP * SLOT, ROWS), 0).astype(F32) == dest
+    hot_f = jnp.where(hot, 1.0, 0.0)
+    oh_v[...] = hot_f.astype(BF)
 
     acc[...] = jnp.zeros_like(acc)
 
@@ -156,20 +170,23 @@
         acc[:, W2:] += mm(rows, vw_v[zc])
         for b in range(4):
             et_v[zc * 4 + b] = blocks[b].T
+
+    def distribute(zc):
         xc = zc // 2
         half = zc % 2
         to_line(
-            et_v.at[pl.ds(zc * 4, 4)], el.at[x * 2 + c, pl.ds(half * 4, 4)],
+            zc, et_v.at[pl.ds(zc * 4, 4)], el.at[x * 2 + c, pl.ds(half * 4, 4)],
             (xc * 8 + y * 2, z), (xc == x) & (c == 0),
         )
         for j in range(2):
             yc = half * 2 + j
             to_line(
-                et_v.at[pl.ds(zc * 4 + 2 * j, 2)], el.at[y * 2 + c, pl.ds(xc * 2, 2)],
+                zc, et_v.at[pl.ds(zc * 4 + 2 * j, 2)], el.at[y * 2 + c, pl.ds(xc * 2, 2)],
                 (x * 8 + yc * 2 + 1, z), (yc == y) & (c == 1),
             )
 
     process(z)
+    distribute(z)
 
     def gather_step(k, carry):
         for direction, part in travel:
@@ -178,14 +195,43 @@
                 z_copy(direction, k + 1, part).start()
             else:
                 pl.when(k < 3)(z_copy(direction, k + 1, part).start)
-        process((z + NZ - k) % NZ)
-        process((z + k) % NZ)
+        for zc in ((z + NZ - k) % NZ, (z + k) % NZ):
+            process(zc)
+            pl.when(k < FAR)(lambda: distribute(zc))
         return carry
 
     lax.fori_loop(1, 4, gather_step, 0)
     for direction, part in travel[:4]:
         z_copy(direction, 4, part).wait_recv()
     process((z + 4) % NZ)
+
+    def line_blocks(zc, core):
+        return pl.ds((zc % 2) * 4, 4) if core == 0 else pl.ds((zc // 2) * 2, 2)
+
+    def on_holder(zc, fn):
+        pl.when((c == 0) & (zc // 2 == x))(lambda: fn(0))
+        pl.when((c == 1) & (zc % 2 == y // 2))(lambda: fn(1))
+
+    def wait_line(zc):
+        def one(core):
+            drained(el.at[:, line_blocks(zc, core)], el_recv.at[zc])
+
+        on_holder(zc, one)
+
+    def along_z(n, act):
+        zc, step, first, count = (
+            (z + 2, 7, 0, 8), (z + 6, 1, 0, 8),
+        )[n]
+        zc = zc % NZ
+
+        def one(core):
+            at = el.at[pl.ds(first, count), line_blocks(zc, core)]
+            act(pltpu.make_async_remote_copy(
+                src_ref=at, dst_ref=at, send_sem=elz_send.at[n], recv_sem=el_recv.at[zc],
+                device_id=(d, (z + step) % NZ), device_id_type=MESH,
+            ))
+
+        on_holder(zc, one)
 
     def exchange(src, dst, send_sem, recv_sem, h):
         mine = pl.ds(pl.multiple_of(d * SLOT, SLOT), SLOT)
@@ -206,9 +252,6 @@
 
         lax.fori_loop(1, NDP, send, 0)
 
-    def drained(buf, sem):
-        pltpu.make_async_copy(buf, buf, sem).wait()
-
     most = pl.ds(0, (NDP - 1) * SLOT)
     hot_b = oh_v[...]
     dead = jnp.sum(hot_b.astype(F32), axis=1, keepdims=True) < 0.5
@@ -218,8 +261,15 @@
         slots[h, :, :HD] = jnp.where(dead, DEAD, keys).astype(BF)
         slots[h, :, HD:] = mm(hot_b, acc[:, pl.ds(W2 + h * HD, HD)].astype(BF)).astype(BF)
         exchange(slots, kvr, kv_send, kv_recv, h)
+    distribute((z + 4) % NZ)
+
+    for k in (2, 6):
+        wait_line((z + k) % NZ)
+    for n in range(2):
+        along_z(n, lambda copy: copy.start())
 
     n_keys = NDP * SLOT
+    int_copies[2].wait()
     dec_col, dec_before = column_of(dec_len[...].astype(F32), NDP)
     same = iota((NDP, n_keys), 1) // SLOT == iota((NDP, n_keys), 0)
     first = jnp.sum(jnp.where(same, dec_before, 0.0), axis=0, keepdims=True)
@@ -362,7 +412,8 @@
     for direction, part in last_parts:
         rs_part(2, direction, part)
     lax.fori_loop(3, NZ, back_second, 0)
-    drained(el, el_recv)
+    for k in (0, 1, 7, 3, 5, 4):
+        wait_line((z + k) % NZ)
     partial_blocks(0)
     for direction, part in first_parts:
         rs_part(2, direction, part)
@@ -400,7 +451,16 @@
                     z_copy(direction, step, part).wait_send()
                 if step > 1 or near(direction, part):
                     rs_copy(direction, step, part).wait_send()
-    drained(el.at[pl.ds(0, 7)], el_send)
+    for k in (0, 1, 7, 2, 6, 4):
+        zc = (z + k) % NZ
+        own_x = (c == 0) & (zc // 2 == x)
+        own_y = (c == 1) & (zc % 2 == y // 2)
+        pl.when(own_x)(lambda: drained(et_v.at[pl.ds(0, 4)], el_send.at[zc]))
+        pl.when(own_y)(lambda: drained(et_v.at[pl.ds(0, 6)], el_send.at[zc]))
+        other = jnp.logical_not(own_x | own_y)
+        pl.when(other)(lambda: drained(et_v.at[pl.ds(0, 8)], el_send.at[zc]))
+    for n in range(2):
+        along_z(n, lambda copy: copy.wait_send())
     for h in range(2):
         drained(kvr.at[h, most], kv_send.at[h])
         drained(gr.at[h, most], g_send.at[h])
@@ -428,7 +488,6 @@
 
 def body(queries, enc_rows, key_weight, value_weight, enc_len, dec_len, route, out_grad):
     any_spec = pl.BlockSpec(memory_space=pl.ANY)
-    small = pl.BlockSpec(memory_space=pltpu.VMEM)
     dma = pltpu.SemaphoreType.DMA
     results = (
         jax.ShapeDtypeStruct((DEC, W2), BF),
@@ -440,7 +499,7 @@
     made = pl.pallas_call(
         kernel,
         out_shape=results,
-        in_specs=[any_spec] * 4 + [small] * 3 + [any_spec],
+        in_specs=[any_spec] * 8,
         out_specs=[any_spec] * 5,
         scratch_shapes=[
             pltpu.VMEM((32, 128, 128), BF),
@@ -467,13 +526,17 @@
             pltpu.VMEM((DEC, W2), BF),
             pltpu.VMEM((ROWS, W2), BF),
             pltpu.VMEM((2, ROWS, W2), F32),
+            pltpu.VMEM((1, NDP), jnp.int32),
+            pltpu.VMEM((1, NDP), jnp.int32),
+            pltpu.VMEM((1, NDP), jnp.int32),
             dma(()),
             dma((NZ, 2)),
             dma((2,)),
             dma((2, 4, 4)),
             dma((2, 4, 4)),
-            dma(()),
-            dma(()),
+            dma((NZ,)),
+            dma((NZ,)),
+            dma((2,)),
             dma((2,)),
             dma((2,)),
             dma((2,)),
@@ -485,6 +548,7 @@
             dma((2, 4, 4)),
             dma((2, 4, 4)),
             dma((5,)),
+            dma((3,)),
         ],
         compiler_params=pltpu.CompilerParams(
             collective_id=0, has_side_effects=True, vmem_limit_bytes=60 * 1024 * 1024

time: 83.8 us -> 77.9 us (0.930); the launches traced: 82.8 us -> 77.8 us
  Pallas kernels: 82.1 us -> 77.1 us
    pallas_call x1, Pallas kernels: 80.1 us -> 75.1 us  [body(): pl.pallas_call(kernel, out_shape=results, in_specs=[any_spec] * 8, out_sp...]
where the time goes in v3:
time: 77.9 us; the launch traced here: 77.8 us
  Pallas kernels  77.1 us (99%)
    pallas_call x1, Pallas kernels, body(): pl.pallas_call(kernel, out_shape=results, in_specs=[any_spec] * 8, out_sp...  75.1 us
    pallas_call x1, Pallas kernels, body(): pl.pallas_call(hand_over, out_shape=results, in_specs=[any_spec] * 5, out...  2.04 us

profile of v3, /device:TPU:32, one launch (start us, length us, event | category | flops | bytes accessed | tf_op | source)
XLA Modules:
  0.0 77.8 jit_solution(12325150126729216565)
XLA Ops:
  0.6 75.1 %shard_map.119 = (bf16[256,512]{1,0:T(8,128)(2,1)}, bf16[256,512]{1,0:T(8,128)(2,1)}, bf16[128,512]{1,0:T(8,128)(2,1)}, f32[128,512]{1,0:T(8,128)}, f32[128,512]{1,0:T(8,128)}) custom-call(bf16[256,512]{1,0:T(8,128)(2,1)} %q_hbm.1, bf16[128,512]{1,0:T(8,128)(2,1)} %enc_hbm.1, bf16[4096,512]{1,0:T(8,128)(2,1)} %kw_hbm.1, bf16[4096,512]{1,0:T(8,128)(2,1)} %vw_hbm.1, ...), custom_call_target="tpu_custom_call" | custom-call | tf_op jit(solution)/shard_map/pallas_call | solution.py:499
  75.7 2.0 %shard_map.120 = (bf16[256,512]{1,0:T(8,128)(2,1)}, bf16[256,512]{1,0:T(8,128)(2,1)}, bf16[128,512]{1,0:T(8,128)(2,1)}, f32[128,512]{1,0:T(8,128)}, f32[128,512]{1,0:T(8,128)}) custom-call(bf16[256,512]{1,0:T(8,128)(2,1)} %get-tuple-element.10.refs_0_, bf16[256,512]{1,0:T(8,128)(2,1)} %get-tuple-element.11.refs_1_, ...), custom_call_target="tpu_custom_call" | custom-call | tf_op jit(solution)/shard_map/pallas_call | solution.py:557

commit v4 on v3

--- a/solution.py
+++ b/solution.py
@@ -14,6 +14,7 @@
 W2 = 512
 FAR = 3
 DEAD = 65536.0
+FARTHEST_FIRST = (10, 6, 9, 14, 11, 5, 8, 15, 2, 7, 13, 4, 1, 12, 3)
 MESH = pl.DeviceIdType.MESH
 BF = jnp.bfloat16
 F32 = jnp.float32
@@ -47,7 +48,7 @@
 def kernel(
     q_hbm, enc_hbm, kw_hbm, vw_hbm, enc_len_hbm, dec_len_hbm, route_hbm, og_hbm,
     att_hbm, qg_hbm, eg_hbm, kwg_hbm, vwg_hbm,
-    e_v, et_v, kw_v, vw_v, q_v, og_v, acc, oh_v,
+    e_v, et_v, kw_v, vw_v, q_v, og_v, acc, oh_v, oht_v,
     slots, kvr, gs, gr, gsend, gl, el, ps, cr, dx, rs_s, rs_r,
     att_v, qg_v, eg_v, wg_v, enc_len, dec_len, route,
     enc_sem, w_sem, q_sem, z_send, z_recv, el_send, el_recv, elz_send,
@@ -97,11 +98,6 @@
         w_copy(zc, 1).start()
         return carry
 
-    lax.fori_loop(0, NZ, load_w, 0)
-    q_copy = pltpu.make_async_copy(q_hbm, q_v, q_sem.at[0])
-    og_copy = pltpu.make_async_copy(og_hbm, og_v, q_sem.at[1])
-    q_copy.start()
-    og_copy.start()
     int_copies = [
         pltpu.make_async_copy(src, dst, int_sem.at[i])
         for i, (src, dst) in enumerate(
@@ -133,6 +129,11 @@
     travel = ((0, 0), (1, 3), (0, 1), (1, 2), (0, 2), (1, 1), (0, 3), (1, 0))
     for direction, part in travel:
         z_copy(direction, 1, part).start()
+    lax.fori_loop(0, NZ, load_w, 0)
+    q_copy = pltpu.make_async_copy(q_hbm, q_v, q_sem.at[0])
+    og_copy = pltpu.make_async_copy(og_hbm, og_v, q_sem.at[1])
+    q_copy.start()
+    og_copy.start()
 
     def to_line(zc, src, dst, device, here):
         @pl.when(here)
@@ -238,8 +239,10 @@
         pltpu.make_async_copy(src.at[h, mine], dst.at[h, mine], recv_sem.at[h]).start()
 
         def send(i, carry):
-            o = (i * 11) % NDP
-            t = ((x + o // 8) % 4) * 8 + ((y + (o // 2) % 4) % 4) * 2 + (c + o % 2) % 2
+            o = jnp.int32(0)
+            for n in range(15):
+                o = jnp.where(i // 2 == n, FARTHEST_FIRST[n], o)
+            t = ((x + o // 4) % 4) * 8 + ((y + o % 4) % 4) * 2 + (c + i + 1) % 2
             pltpu.make_async_remote_copy(
                 src_ref=src.at[h, pl.ds(pl.multiple_of(t * SLOT, SLOT), SLOT)],
                 dst_ref=dst.at[h, mine],
@@ -250,7 +253,7 @@
             ).start()
             return carry
 
-        lax.fori_loop(1, NDP, send, 0)
+        lax.fori_loop(0, NDP - 1, send, 0)
 
     most = pl.ds(0, (NDP - 1) * SLOT)
     hot_b = oh_v[...]
@@ -263,10 +266,14 @@
         exchange(slots, kvr, kv_send, kv_recv, h)
     distribute((z + 4) % NZ)
 
-    for k in (2, 6):
-        wait_line((z + k) % NZ)
-    for n in range(2):
-        along_z(n, lambda copy: copy.start())
+    def relay():
+        for k in (2, 6):
+            wait_line((z + k) % NZ)
+        for n in range(2):
+            along_z(n, lambda copy: copy.start())
+
+
+    oht_v[...] = hot_b.T
 
     n_keys = NDP * SLOT
     int_copies[2].wait()
@@ -298,6 +305,8 @@
         gs[h, :, :HD] = mm_tn(ds, q).astype(BF)
         gs[h, :, HD:] = mm_tn(weights, g).astype(BF)
         exchange(gs, gr, g_send, g_recv, h)
+        if h == 0:
+            relay()
         att_v[:, cols] = mm(weights, v).astype(BF)
         qg_v[:, cols] = mm(ds, k).astype(BF)
     att_out = pltpu.make_async_copy(att_v, att_hbm, out_sem.at[0])
@@ -337,7 +346,7 @@
 
     def unpack(h):
         drained(gr.at[h], g_recv.at[h])
-        rows = mm_tn(oh_v[...], gr[h]).astype(BF)
+        rows = mm(oht_v[...], gr[h]).astype(BF)
         gsend[h, 0] = rows[:, :HD]
         gsend[h, 1] = rows[:, HD:]
         spread(h)
@@ -346,29 +355,39 @@
         cols = pl.ds(h * HD, HD)
         return mm_nt(gsend[h, 0], kw_v[zc, :, cols]) + mm_nt(gsend[h, 1], vw_v[zc, :, cols])
 
+    def send_block(h, b):
+        t = jnp.where(c == 0, x * 8 + b, (b // 2) * 8 + y * 2 + b % 2)
+        dst = cr.at[h, c, jnp.where(c == 0, y, x)]
+
+        @pl.when(t == d)
+        def _():
+            pltpu.make_async_copy(ps.at[h, b], dst, c_recv.at[h]).start()
+
+        @pl.when(t != d)
+        def _():
+            pltpu.make_async_remote_copy(
+                src_ref=ps.at[h, b], dst_ref=dst, send_sem=c_send.at[h], recv_sem=c_recv.at[h],
+                device_id=(t, z), device_id_type=MESH,
+            ).start()
+
     def partial_blocks(h):
         drained(gl.at[h], gl_recv.at[h])
 
-        def block(b, carry):
-            lhs = jnp.concatenate([el[j, b] for j in range(8)], axis=1)
-            ps[h, b] = mm(lhs, gl[h]).astype(BF)
-            t = jnp.where(c == 0, x * 8 + b, (b // 2) * 8 + y * 2 + b % 2)
-            dst = cr.at[h, c, jnp.where(c == 0, y, x)]
-
-            @pl.when(t == d)
-            def _():
-                pltpu.make_async_copy(ps.at[h, b], dst, c_recv.at[h]).start()
-
-            @pl.when(t != d)
-            def _():
-                pltpu.make_async_remote_copy(
-                    src_ref=ps.at[h, b], dst_ref=dst, send_sem=c_send.at[h], recv_sem=c_recv.at[h],
-                    device_id=(t, z), device_id_type=MESH,
-                ).start()
-
+        def blocks(n, carry):
+            lhs = jnp.concatenate(
+                [
+                    jnp.concatenate([el[j, n * 4 + i] for j in range(8)], axis=1)
+                    for i in range(4)
+                ],
+                axis=0,
+            )
+            out = mm(lhs, gl[h]).astype(BF)
+            for i in range(4):
+                ps[h, n * 4 + i] = out[i * 128:(i + 1) * 128]
+                send_block(h, n * 4 + i)
             return carry
 
-        lax.fori_loop(0, 8, block, 0)
+        lax.fori_loop(0, 2, blocks, 0)
 
     unpack(0)
 
@@ -510,6 +529,7 @@
             pltpu.VMEM((DEC, W2), BF),
             pltpu.VMEM((ROWS, 2 * W2), F32),
             pltpu.VMEM((NDP * SLOT, ROWS), BF),
+            pltpu.VMEM((ROWS, NDP * SLOT), BF),
             pltpu.VMEM((2, NDP * SLOT, W2), BF),
             pltpu.VMEM((2, NDP * SLOT, W2), BF),
             pltpu.VMEM((2, NDP * SLOT, W2), BF),

time: 77.9 us -> 76.6 us (0.983); the launches traced: 77.8 us -> 75.1 us
  Pallas kernels: 77.1 us -> 74.5 us
    pallas_call x1, Pallas kernels: 75.1 us -> 72.5 us  [body(): pl.pallas_call(kernel, out_shape=results, in_specs=[any_spec] * 8, out_sp...]
where the time goes in v4:
time: 76.6 us; the launch traced here: 75.1 us
  Pallas kernels  74.5 us (97%)
    pallas_call x1, Pallas kernels, body(): pl.pallas_call(kernel, out_shape=results, in_specs=[any_spec] * 8, out_sp...  72.5 us
    pallas_call x1, Pallas kernels, body(): pl.pallas_call(hand_over, out_shape=results, in_specs=[any_spec] * 5, out...  2.04 us

profile of v4, /device:TPU:32, one launch (start us, length us, event | category | flops | bytes accessed | tf_op | source)
XLA Modules:
  0.0 75.1 jit_solution(2570952920885046234)
XLA Ops:
  0.6 72.5 %shard_map.119 = (bf16[256,512]{1,0:T(8,128)(2,1)}, bf16[256,512]{1,0:T(8,128)(2,1)}, bf16[128,512]{1,0:T(8,128)(2,1)}, f32[128,512]{1,0:T(8,128)}, f32[128,512]{1,0:T(8,128)}) custom-call(bf16[256,512]{1,0:T(8,128)(2,1)} %q_hbm.1, bf16[128,512]{1,0:T(8,128)(2,1)} %enc_hbm.1, bf16[4096,512]{1,0:T(8,128)(2,1)} %kw_hbm.1, bf16[4096,512]{1,0:T(8,128)(2,1)} %vw_hbm.1, ...), custom_call_target="tpu_custom_call" | custom-call | tf_op jit(solution)/shard_map/pallas_call | solution.py:518
  73.1 2.0 %shard_map.120 = (bf16[256,512]{1,0:T(8,128)(2,1)}, bf16[256,512]{1,0:T(8,128)(2,1)}, bf16[128,512]{1,0:T(8,128)(2,1)}, f32[128,512]{1,0:T(8,128)}, f32[128,512]{1,0:T(8,128)}) custom-call(bf16[256,512]{1,0:T(8,128)(2,1)} %get-tuple-element.10.refs_0_, bf16[256,512]{1,0:T(8,128)(2,1)} %get-tuple-element.11.refs_1_, ...), custom_call_target="tpu_custom_call" | custom-call | tf_op jit(solution)/shard_map/pallas_call | solution.py:577

commit v5 on v4

--- a/solution.py
+++ b/solution.py
@@ -77,7 +77,7 @@
         ).start()
 
     barrier = pltpu.get_barrier_semaphore()
-    for peer in ring:
+    for peer in (*ring, (d, (z + 2) % NZ), (d, (z + NZ - 2) % NZ)):
         pl.semaphore_signal(barrier, inc=1, device_id=peer, device_id_type=MESH)
 
     def greet(i, carry):
@@ -107,7 +107,7 @@
     for copy in int_copies:
         copy.start()
 
-    pl.semaphore_wait(barrier, NDP + 1)
+    pl.semaphore_wait(barrier, NDP + 3)
     pltpu.make_async_copy(e_v.at[pl.ds(0, 4)], e_v.at[pl.ds(z * 4, 4)], enc_sem).wait()
 
     def z_copy(direction, step, part):
@@ -176,13 +176,13 @@
         xc = zc // 2
         half = zc % 2
         to_line(
-            zc, et_v.at[pl.ds(zc * 4, 4)], el.at[x * 2 + c, pl.ds(half * 4, 4)],
+            zc, et_v.at[pl.ds(zc * 4, 4)], el.at[c * 4 + x, pl.ds(half * 4, 4)],
             (xc * 8 + y * 2, z), (xc == x) & (c == 0),
         )
         for j in range(2):
             yc = half * 2 + j
             to_line(
-                zc, et_v.at[pl.ds(zc * 4 + 2 * j, 2)], el.at[y * 2 + c, pl.ds(xc * 2, 2)],
+                zc, et_v.at[pl.ds(zc * 4 + 2 * j, 2)], el.at[c * 4 + y, pl.ds(xc * 2, 2)],
                 (x * 8 + yc * 2 + 1, z), (yc == y) & (c == 1),
             )
 
@@ -221,7 +221,7 @@
 
     def along_z(n, act):
         zc, step, first, count = (
-            (z + 2, 7, 0, 8), (z + 6, 1, 0, 8),
+            (z + 2, 7, 0, 8), (z + 6, 1, 0, 8), (z + 2, 6, 4, 2), (z + 6, 2, 6, 2),
         )[n]
         zc = zc % NZ
 
@@ -264,15 +264,16 @@
         slots[h, :, :HD] = jnp.where(dead, DEAD, keys).astype(BF)
         slots[h, :, HD:] = mm(hot_b, acc[:, pl.ds(W2 + h * HD, HD)].astype(BF)).astype(BF)
         exchange(slots, kvr, kv_send, kv_recv, h)
-    distribute((z + 4) % NZ)
+    pl.when(c == 0)(lambda: distribute((z + 4) % NZ))
 
     def relay():
         for k in (2, 6):
             wait_line((z + k) % NZ)
-        for n in range(2):
+        for n in range(4):
             along_z(n, lambda copy: copy.start())
 
 
+    relay()
     oht_v[...] = hot_b.T
 
     n_keys = NDP * SLOT
@@ -305,8 +306,6 @@
         gs[h, :, :HD] = mm_tn(ds, q).astype(BF)
         gs[h, :, HD:] = mm_tn(weights, g).astype(BF)
         exchange(gs, gr, g_send, g_recv, h)
-        if h == 0:
-            relay()
         att_v[:, cols] = mm(weights, v).astype(BF)
         qg_v[:, cols] = mm(ds, k).astype(BF)
     att_out = pltpu.make_async_copy(att_v, att_hbm, out_sem.at[0])
@@ -318,10 +317,10 @@
         def one(kv, i):
             if kv == 0:
                 t = ((x + i) % 4) * 8 + y * 2
-                at = x * 2 + c
+                at = c * 4 + x
             else:
                 t = x * 8 + ((y + i) % 4) * 2 + 1
-                at = y * 2 + c
+                at = c * 4 + y
             src = gsend.at[h, kv]
             dst = gl.at[h, pl.ds(pl.multiple_of(at * ROWS, ROWS), ROWS)]
 
@@ -474,11 +473,12 @@
         zc = (z + k) % NZ
         own_x = (c == 0) & (zc // 2 == x)
         own_y = (c == 1) & (zc % 2 == y // 2)
-        pl.when(own_x)(lambda: drained(et_v.at[pl.ds(0, 4)], el_send.at[zc]))
-        pl.when(own_y)(lambda: drained(et_v.at[pl.ds(0, 6)], el_send.at[zc]))
+        sent = (c == 0) | (k != 4)
         other = jnp.logical_not(own_x | own_y)
-        pl.when(other)(lambda: drained(et_v.at[pl.ds(0, 8)], el_send.at[zc]))
-    for n in range(2):
+        pl.when(sent & own_x)(lambda: drained(et_v.at[pl.ds(0, 4)], el_send.at[zc]))
+        pl.when(sent & own_y)(lambda: drained(et_v.at[pl.ds(0, 6)], el_send.at[zc]))
+        pl.when(sent & other)(lambda: drained(et_v.at[pl.ds(0, 8)], el_send.at[zc]))
+    for n in range(4):
         along_z(n, lambda copy: copy.wait_send())
     for h in range(2):
         drained(kvr.at[h, most], kv_send.at[h])
@@ -556,7 +556,7 @@
             dma((2, 4, 4)),
             dma((NZ,)),
             dma((NZ,)),
-            dma((2,)),
+            dma((4,)),
             dma((2,)),
             dma((2,)),
             dma((2,)),

time: 76.6 us -> 72.9 us (0.952); the launches traced: 75.1 us -> 72.8 us
  Pallas kernels: 74.5 us -> 72.2 us
    pallas_call x1, Pallas kernels: 72.5 us -> 70.1 us  [body(): pl.pallas_call(kernel, out_shape=results, in_specs=[any_spec] * 8, out_sp...]
where the time goes in v5:
time: 72.9 us; the launch traced here: 72.8 us
  Pallas kernels  72.2 us (99%)
    pallas_call x1, Pallas kernels, body(): pl.pallas_call(kernel, out_shape=results, in_specs=[any_spec] * 8, out_sp...  70.1 us
    pallas_call x1, Pallas kernels, body(): pl.pallas_call(hand_over, out_shape=results, in_specs=[any_spec] * 5, out...  2.04 us

profile of v5, /device:TPU:32, one launch (start us, length us, event | category | flops | bytes accessed | tf_op | source)
XLA Modules:
  0.0 72.8 jit_solution(9881767883001821981)
XLA Ops:
  0.6 70.1 %shard_map.119 = (bf16[256,512]{1,0:T(8,128)(2,1)}, bf16[256,512]{1,0:T(8,128)(2,1)}, bf16[128,512]{1,0:T(8,128)(2,1)}, f32[128,512]{1,0:T(8,128)}, f32[128,512]{1,0:T(8,128)}) custom-call(bf16[256,512]{1,0:T(8,128)(2,1)} %q_hbm.1, bf16[128,512]{1,0:T(8,128)(2,1)} %enc_hbm.1, bf16[4096,512]{1,0:T(8,128)(2,1)} %kw_hbm.1, bf16[4096,512]{1,0:T(8,128)(2,1)} %vw_hbm.1, ...), custom_call_target="tpu_custom_call" | custom-call | tf_op jit(solution)/shard_map/pallas_call | solution.py:518
  70.8 2.0 %shard_map.120 = (bf16[256,512]{1,0:T(8,128)(2,1)}, bf16[256,512]{1,0:T(8,128)(2,1)}, bf16[128,512]{1,0:T(8,128)(2,1)}, f32[128,512]{1,0:T(8,128)}, f32[128,512]{1,0:T(8,128)}) custom-call(bf16[256,512]{1,0:T(8,128)(2,1)} %get-tuple-element.10.refs_0_, bf16[256,512]{1,0:T(8,128)(2,1)} %get-tuple-element.11.refs_1_, ...), custom_call_target="tpu_custom_call" | custom-call | tf_op jit(solution)/shard_map/pallas_call | solution.py:577

commit v6 on v5

--- a/solution.py
+++ b/solution.py
@@ -169,8 +169,10 @@
         w_copy(zc, 1).wait()
         acc[:, :W2] += mm(rows, kw_v[zc])
         acc[:, W2:] += mm(rows, vw_v[zc])
+
+    def turn(zc):
         for b in range(4):
-            et_v[zc * 4 + b] = blocks[b].T
+            et_v[zc * 4 + b] = e_v[zc * 4 + b].T
 
     def distribute(zc):
         xc = zc // 2
@@ -187,6 +189,7 @@
             )
 
     process(z)
+    turn(z)
     distribute(z)
 
     def gather_step(k, carry):
@@ -198,6 +201,7 @@
                 pl.when(k < 3)(z_copy(direction, k + 1, part).start)
         for zc in ((z + NZ - k) % NZ, (z + k) % NZ):
             process(zc)
+            turn(zc)
             pl.when(k < FAR)(lambda: distribute(zc))
         return carry
 
@@ -264,6 +268,7 @@
         slots[h, :, :HD] = jnp.where(dead, DEAD, keys).astype(BF)
         slots[h, :, HD:] = mm(hot_b, acc[:, pl.ds(W2 + h * HD, HD)].astype(BF)).astype(BF)
         exchange(slots, kvr, kv_send, kv_recv, h)
+    turn((z + 4) % NZ)
     pl.when(c == 0)(lambda: distribute((z + 4) % NZ))
 
     def relay():
@@ -352,7 +357,9 @@
 
     def back(h, zc):
         cols = pl.ds(h * HD, HD)
-        return mm_nt(gsend[h, 0], kw_v[zc, :, cols]) + mm_nt(gsend[h, 1], vw_v[zc, :, cols])
+        grads = jnp.concatenate([gsend[h, 0], gsend[h, 1]], axis=1)
+        weights = jnp.concatenate([kw_v[zc, :, cols], vw_v[zc, :, cols]], axis=1)
+        return mm_nt(grads, weights)
 
     def send_block(h, b):
         t = jnp.where(c == 0, x * 8 + b, (b // 2) * 8 + y * 2 + b % 2)

time: 72.9 us -> 73.6 us (level); the launches traced: 72.8 us -> 72.3 us
  no operation moved by 1% of the time
where the time goes in v6:
time: 73.6 us; the launch traced here: 72.3 us
  Pallas kernels  71.6 us (97%)
    pallas_call x1, Pallas kernels, body(): pl.pallas_call(kernel, out_shape=results, in_specs=[any_spec] * 8, out_sp...  69.6 us
    pallas_call x1, Pallas kernels, body(): pl.pallas_call(hand_over, out_shape=results, in_specs=[any_spec] * 5, out...  2.04 us

profile of v6, /device:TPU:32, one launch (start us, length us, event | category | flops | bytes accessed | tf_op | source)
XLA Modules:
  0.0 72.3 jit_solution(2853035821169461358)
XLA Ops:
  0.6 69.6 %shard_map.119 = (bf16[256,512]{1,0:T(8,128)(2,1)}, bf16[256,512]{1,0:T(8,128)(2,1)}, bf16[128,512]{1,0:T(8,128)(2,1)}, f32[128,512]{1,0:T(8,128)}, f32[128,512]{1,0:T(8,128)}) custom-call(bf16[256,512]{1,0:T(8,128)(2,1)} %q_hbm.1, bf16[128,512]{1,0:T(8,128)(2,1)} %enc_hbm.1, bf16[4096,512]{1,0:T(8,128)(2,1)} %kw_hbm.1, bf16[4096,512]{1,0:T(8,128)(2,1)} %vw_hbm.1, ...), custom_call_target="tpu_custom_call" | custom-call | tf_op jit(solution)/shard_map/pallas_call | solution.py:525
  70.2 2.0 %shard_map.120 = (bf16[256,512]{1,0:T(8,128)(2,1)}, bf16[256,512]{1,0:T(8,128)(2,1)}, bf16[128,512]{1,0:T(8,128)(2,1)}, f32[128,512]{1,0:T(8,128)}, f32[128,512]{1,0:T(8,128)}) custom-call(bf16[256,512]{1,0:T(8,128)(2,1)} %get-tuple-element.10.refs_0_, bf16[256,512]{1,0:T(8,128)(2,1)} %get-tuple-element.11.refs_1_, ...), custom_call_target="tpu_custom_call" | custom-call | tf_op jit(solution)/shard_map/pallas_call | solution.py:584

commit v7 on v5

--- a/solution.py
+++ b/solution.py
@@ -264,7 +264,6 @@
         slots[h, :, :HD] = jnp.where(dead, DEAD, keys).astype(BF)
         slots[h, :, HD:] = mm(hot_b, acc[:, pl.ds(W2 + h * HD, HD)].astype(BF)).astype(BF)
         exchange(slots, kvr, kv_send, kv_recv, h)
-    pl.when(c == 0)(lambda: distribute((z + 4) % NZ))
 
     def relay():
         for k in (2, 6):
@@ -274,6 +273,7 @@
 
 
     relay()
+    pl.when(c == 0)(lambda: distribute((z + 4) % NZ))
     oht_v[...] = hot_b.T
 
     n_keys = NDP * SLOT

time: 72.9 us -> 72.9 us (level)
  no operation moved by 1% of the time
where the time goes in v7:
time: 72.9 us; the launch traced here: 72.8 us
  Pallas kernels  72.2 us (99%)
    pallas_call x1, Pallas kernels, body(): pl.pallas_call(kernel, out_shape=results, in_specs=[any_spec] * 8, out_sp...  70.1 us
    pallas_call x1, Pallas kernels, body(): pl.pallas_call(hand_over, out_shape=results, in_specs=[any_spec] * 5, out...  2.04 us

profile of v7, /device:TPU:32, one launch (start us, length us, event | category | flops | bytes accessed | tf_op | source)
XLA Modules:
  0.0 72.8 jit_solution(13562259601281139845)
XLA Ops:
  0.6 70.1 %shard_map.119 = (bf16[256,512]{1,0:T(8,128)(2,1)}, bf16[256,512]{1,0:T(8,128)(2,1)}, bf16[128,512]{1,0:T(8,128)(2,1)}, f32[128,512]{1,0:T(8,128)}, f32[128,512]{1,0:T(8,128)}) custom-call(bf16[256,512]{1,0:T(8,128)(2,1)} %q_hbm.1, bf16[128,512]{1,0:T(8,128)(2,1)} %enc_hbm.1, bf16[4096,512]{1,0:T(8,128)(2,1)} %kw_hbm.1, bf16[4096,512]{1,0:T(8,128)(2,1)} %vw_hbm.1, ...), custom_call_target="tpu_custom_call" | custom-call | tf_op jit(solution)/shard_map/pallas_call | solution.py:518
  70.8 2.0 %shard_map.120 = (bf16[256,512]{1,0:T(8,128)(2,1)}, bf16[256,512]{1,0:T(8,128)(2,1)}, bf16[128,512]{1,0:T(8,128)(2,1)}, f32[128,512]{1,0:T(8,128)}, f32[128,512]{1,0:T(8,128)}) custom-call(bf16[256,512]{1,0:T(8,128)(2,1)} %get-tuple-element.10.refs_0_, bf16[256,512]{1,0:T(8,128)(2,1)} %get-tuple-element.11.refs_1_, ...), custom_call_target="tpu_custom_call" | custom-call | tf_op jit(solution)/shard_map/pallas_call | solution.py:577
